TPU v7x, 256 devices: a whole 4x4x8 slice. The times are simulated.
256 devices in a mesh: dp: 32 (over z, y_hi, core), tensor: 8 (over y_lo, x).
Axes of the slice: x: 4, y: 4 (y_hi: 2, y_lo: 2; y = y_hi * 2 + y_lo), z: 8, core: 2. Of those that a mesh axis runs over, the one named last changes fastest.
Arguments:
- hidden: bfloat16 [16384, 24576], P('dp', 'tensor'), may hold values from -6 to 6
- down_grad: bfloat16 [24576, 6144], P('tensor', 'dp'), may hold values from -6 to 6
- old_inverse: float32 [8, 3072, 768], P('tensor', 'dp'), may hold values from -1 to 1
- owner: int32 [8, 4], P('tensor'), may hold values from 0 to 3, each once within a row
- damping: float32 [], replicated, may hold values from 0.05 to 0.5
Outputs:
- preconditioned: bfloat16 [24576, 6144], P('tensor', 'dp')
- new_inverse: float32 [8, 3072, 768], P('tensor', 'dp')
All inputs are finite; a program needn't handle non-finite values.
Results may differ from a plain program's by a relative error of at most 0.02.
Values may be sent and summed in bfloat16 or wider, within the bound.
A program may use at most 64 MiB of HBM per device.

v0:
```python
import jax
import jax.numpy as jnp
from jax import lax
from jax.experimental import pallas as pl
from jax.experimental.pallas import tpu as pltpu
from jax.sharding import PartitionSpec as P

MESH = pl.DeviceIdType.MESH
B = 768
T = 128
NT = B // T
PACK = (NT * (NT - 1) // 2 + NT // 2 + 1) * T
Z = 8
SHARD = PACK // Z
WROWS = 96
WCUT = 48
COLS = 192
TOKENS = 16384
N_MSG = 140
WARM = ((0, 48, 32), (48, 48, 16))
BF = jnp.bfloat16
F32 = jnp.float32


def dot(a, b):
    return jnp.dot(a, b, preferred_element_type=F32)


def tile_rows(bi, bj):
    start = (bi * (bi - 1) // 2 + bj) * T
    return slice(start, start + T)


def fold_rows(i):
    start = (NT * (NT - 1) // 2 + i) * T
    return slice(start, start + T)


LAST = fold_rows(NT // 2)


PIECES = (((0, 160, 80), (160, 144, 64)), ((0, 160, 80), (160, 144, 64)))
PLAN = (
    "G0", "bar", "P0", "W", "V", "grad", "G1", "P1", "G2", "S0", "ab", "G3", "S1", "W", "ab", "cd", "V",
    "ab", "cd", "W", "ab", "cd", "V", "ab", "cd", "W", "ab", "cd", "V", "ab", "cd", "W", "V", "ab", "cd",
    "gw", "W", "V", "ab", "cd", "x", "AA", "cd", "AAAAA", "cd", "BBB", "N", "BBBB", "N", "N",
)


def nt_dot(a, b):
    return lax.dot_general(a, b, (((1,), (1,)), ((), ())), preferred_element_type=F32)


def kernel(
    owner, damping, hid, grad, old, out, inv,
    h, pf, ps, pr, rs_s, rs_r, col, ys, yr, spk, w, wf, sf, x0, q1, q2, gt, av, w1, wb, yt,
    g0, inv_s, inv_r, inv_o, loc, send, recv,
):
    me = lax.axis_index("dp")
    tens = lax.axis_index("tensor")
    z, yh, c = me // 4, me // 2 % 2, me % 2

    def ring(shift):
        return lax.rem(z + shift % Z, Z)

    up = (ring(1) * 4 + yh * 2 + c, tens)
    down = (ring(-1) * 4 + yh * 2 + c, tens)
    across = (z * 4 + (1 - yh) * 2 + c, tens)
    sib = (z * 4 + yh * 2 + 1 - c, tens)
    dirs = (down, up)
    sent = []

    class Message:
        def __init__(self, src, dst, device, land=None):
            n = len(sent)
            self.copy = pltpu.make_async_remote_copy(
                src_ref=src, dst_ref=dst, send_sem=send.at[n], recv_sem=recv.at[n], device_id=device, device_id_type=MESH
            )
            land = dst if land is None else land
            self.arrival = pltpu.make_async_remote_copy(
                src_ref=land, dst_ref=land, send_sem=send.at[n], recv_sem=recv.at[n], device_id=device, device_id_type=MESH
            )
            self.arrived = False
            self.copy.start()
            sent.append(self)

        def wait(self):
            self.arrived = True
            self.arrival.wait_recv()

    class Load:
        def __init__(self, src, dst, n):
            self.copy = pltpu.make_async_copy(src, dst, loc.at[n])
            self.copy.start()
            self.waited = False
            loads.append(self)

        def wait(self):
            self.waited = True
            self.copy.wait()

    loads = []
    hid_copies = []
    for q in range(4):
        block = 2 * (1 - c) + q if q < 2 else 2 * c + q - 2
        hid_copies.append(Load(hid.at[:, pl.ds(pl.multiple_of(block * B, B), B)], h.at[q], q))
    old_copy = Load(old.at[0], wf, 4)

    def columns(core, j):
        return pl.ds(pl.multiple_of((2 * core + j) * B, B), B)

    grad_copies = [Load(grad.at[:, columns(c, j)], gt.at[j, 0:COLS], 5 + j) for j in range(2)]

    barrier = pltpu.get_barrier_semaphore()
    for device in (up, down, across, sib):
        pl.semaphore_signal(barrier, inc=1, device_id=device, device_id_type=MESH)

    row = lax.broadcasted_iota(jnp.int32, (T, T), 0)
    column = lax.broadcasted_iota(jnp.int32, (T, T), 1)

    def gram(q):
        hid_copies[q].wait()

        def put(rows, tile):
            if q < 2:
                ps[q, rows, :] = tile.astype(BF)
            else:
                pf[q - 2, rows, :] = tile

        last = jnp.zeros((T, T), F32)
        for i in range(B // 256):
            left = h[q, :, 256 * i : 256 * i + 256].T
            block = dot(left, h[q, :, 0 : 256 * i + 256])
            for a in range(2):
                bi = 2 * i + a
                for bj in range(bi):
                    put(tile_rows(bi, bj), block[T * a : T * a + T, T * bj : T * bj + T])
            lower = block[0:T, 256 * i : 256 * i + T]
            upper = block[T:, 256 * i + T :]
            put(fold_rows(i), jnp.where(row >= column, lower, upper))
            last = jnp.where(row == i, jnp.sum(jnp.where(row == column, upper, 0.0), axis=0, keepdims=True), last)
        put(LAST, last)

    def warm(lo, size, cut):
        every = slice(lo, lo + size)

        def cross(origin):
            return Message(w.at[origin, yh, c, every], w.at[origin, yh, c, every], across, land=w.at[origin, 1 - yh, c, every])

        def step(t):
            messages = []
            for d, sign in ((0, -1), (1, 1)):
                origin, arriving = ring(-sign * (t - 1)), ring(-sign * t)
                rows = every if t < 4 else (slice(lo, lo + cut), slice(lo + cut, lo + size))[d]
                messages.append(
                    Message(w.at[origin, yh, c, rows], w.at[origin, yh, c, rows], dirs[d], land=w.at[arriving, yh, c, rows])
                )
            return messages

        ringed = step(1)
        crossed = [cross(z)]
        yield
        for t in (2, 3, 4):
            for m in ringed:
                m.wait()
            ringed = step(t)
            crossed += [cross(ring(1 - t)), cross(ring(t - 1))]
            yield
        for m in ringed:
            m.wait()
        crossed.append(cross(ring(4)))
        swapped = [Message(w.at[:, yh, c, every], w.at[:, yh, c, every], sib, land=w.at[:, yh, 1 - c, every])]
        yield
        for m in crossed:
            m.wait()
        swapped.append(
            Message(w.at[:, 1 - yh, c, every], w.at[:, 1 - yh, c, every], sib, land=w.at[:, 1 - yh, 1 - c, every])
        )
        yield
        for m in swapped:
            m.wait()
        yield

    def stream(j, lo, size, cut):
        def rows_of(dest, first=0, count=size):
            return pl.ds(pl.multiple_of(dest * SHARD + lo + first, 16), count)

        def own(dest):
            rows = rows_of(dest)
            return pf[j, rows, :] + pr[j, rows, :].astype(F32)

        here = slice(lo, lo + size)
        halves = (slice(0, cut), slice(cut, size))
        placed = (slice(lo, lo + cut), slice(lo + cut, lo + size))
        part = own(ring(4)).astype(BF)
        before = []
        for d in range(2):
            rs_s[j, d, 0, placed[d], :] = part[halves[d]]
            before.append(Message(rs_s.at[j, d, 0, placed[d]], rs_r.at[j, d, 0, placed[d]], dirs[d]))
        yield
        for t in (2, 3, 4):
            after = []
            for d, sign in ((0, -1), (1, 1)):
                part = own(ring(sign * (5 - t)))
                before[d].wait()
                if t == 2:
                    rs_s[j, d, 1, placed[1 - d], :] = part[halves[1 - d]].astype(BF)
                    rs_s[j, d, 1, placed[d], :] = (part[halves[d]] + rs_r[j, d, 0, placed[d], :].astype(F32)).astype(BF)
                else:
                    rs_s[j, d, t - 1, here, :] = (part + rs_r[j, d, t - 2, here, :].astype(F32)).astype(BF)
                after.append(Message(rs_s.at[j, d, t - 1, here], rs_r.at[j, d, t - 1, here], dirs[d]))
            before = after
            yield
        part = own(z)
        for d in range(2):
            before[d].wait()
            part = part + rs_r[j, d, 3, here, :].astype(F32)
        col[j, here, :] = part
        ys[j, here, :] = part.astype(BF)
        crossed = Message(ys.at[j, here], yr.at[j, here], across)
        yield
        crossed.wait()
        spk[j, rows_of(z), :] = (col[j, here, :] + yr[j, here, :].astype(F32)).astype(BF)
        for t in (1, 2, 3, 4):
            after = []
            for d, sign in ((0, -1), (1, 1)):
                if t > 1:
                    before[d].wait()
                origin, arriving = ring(-sign * (t - 1)), ring(-sign * t)
                first, count = (0, size) if t < 4 else ((0, cut), (cut, size - cut))[d]
                src, land = rows_of(origin, first, count), rows_of(arriving, first, count)
                after.append(Message(spk.at[j, src], spk.at[j, src], dirs[d], land=spk.at[j, land]))
            before = after
            yield
        for m in before:
            m.wait()
        yield

    damp = damping[0, 0]
    tail = {}
    first_row = (z % 2) * 4 * WROWS + yh * 2 * WROWS

    def prepare():
        for name in "WV":
            for _ in runs.get(name, ()):
                pass
        for j in range(2):
            slot = owner[0, 2 * c + j]
            x0[j] = w[pl.ds(2 * slot, 2)].reshape(B, B)
        for j in range(2):
            g0[j] = nt_dot(gt[j], x0[j])

    def refine(j):
        for name in piece_names[j]:
            for _ in runs.get(name, ()):
                pass
        for bi in range(NT):
            for bj in range(bi):
                tile = spk[j, tile_rows(bi, bj), :]
                sf[T * bi : T * bi + T, T * bj : T * bj + T] = tile
                sf[T * bj : T * bj + T, T * bi : T * bi + T] = tile.T
        last = spk[j, LAST, :].astype(F32)
        for i in range(NT // 2):
            tile = spk[j, fold_rows(i), :].astype(F32)
            turned = tile.T
            at = slice(256 * i, 256 * i + T)
            sf[at, at] = jnp.where(row >= column, tile, turned).astype(BF)
            at = slice(256 * i + T, 256 * i + 256)
            rest = jnp.where(row > column, turned, last[i : i + 1, :])
            sf[at, at] = jnp.where(row < column, tile, rest).astype(BF)
        yield
        product = dot(x0[j], sf[...])
        diagonal = lax.broadcasted_iota(jnp.int32, (B, B), 0) == lax.broadcasted_iota(jnp.int32, (B, B), 1)
        left = jnp.where(diagonal, 1.0, 0.0) - product * (1.0 / TOKENS) - damp * x0[j].astype(F32)
        q1[j] = left.astype(BF)
        yield
        q2[j] = dot(q1[j], q1[j]).astype(BF)
        yield
        first = g0[j] + nt_dot(g0[j].astype(BF), q1[j])
        w1[...] = first
        wb[...] = first.astype(BF)
        yield
        second = w1[...] + nt_dot(wb[...], q2[j])
        w1[...] = second
        av[...] = second.astype(BF)
        yield
        wb[...] = nt_dot(av[...], q2[j]).astype(BF)
        yield
        yt[j] = (w1[...] + nt_dot(wb[...], q2[j])).astype(BF)
        store = pltpu.make_async_copy(yt.at[j, 0:COLS], out.at[:, columns(c, j)], loc.at[7 + j])
        store.start()
        tail[j] = store, Message(
            yt.at[j, COLS : 2 * COLS], out.at[:, columns(c, j)], sib, land=out.at[:, columns(1 - c, j)]
        )
        yield

    def inverse_rows():
        slot = z // 2
        block = jnp.int32(0)
        for k in range(4):
            block = jnp.where(owner[0, k] == slot, k, block)
        jj = block % 2
        shape = (2 * WROWS, B)
        unit = lax.broadcasted_iota(jnp.int32, shape, 0) + first_row == lax.broadcasted_iota(jnp.int32, shape, 1)
        mine = q1[jj, pl.ds(pl.multiple_of(first_row, 2 * WROWS), 2 * WROWS), :]
        u = jnp.where(unit, 1.0, 0.0) + mine.astype(F32)
        u = u + dot(u.astype(BF), q2[jj])
        v = dot(u.astype(BF), q2[jj])
        u = u + dot(v.astype(BF), q2[jj])
        inv_s[...] = dot(u.astype(BF), x0[jj])
        message = Message(inv_s.at[pl.ds(pl.multiple_of((1 - c) * WROWS, WROWS), WROWS)], inv_r, sib)
        yield
        message.wait()
        own_part = inv_s[pl.ds(pl.multiple_of(c * WROWS, WROWS), WROWS), :]
        inv_o[...] = jnp.where(block // 2 == c, own_part, inv_r[...])
        store = pltpu.make_async_copy(inv_o, inv.at[0], loc.at[9])
        store.start()
        yield
        store.wait()
        yield

    runs = {"N": inverse_rows(), "A": refine(0), "B": refine(1)}
    piece_names = ("ab", "cd")
    for name, piece in zip("WV", WARM):
        runs[name] = warm(*piece)
    for j in range(2):
        for name, piece in zip(piece_names[j], PIECES[j]):
            runs[name] = stream(j, *piece)
    stat = []
    for step in PLAN:
        if step[0] == "G":
            gram(int(step[1]))
        elif step[0] == "P":
            q = int(step[1])
            stat.append(Message(ps.at[q], pr.at[q], sib))
        elif step == "bar":
            pl.semaphore_wait(barrier, 4)
            old_copy.wait()
            w[z, yh, c] = wf[...].astype(BF)
        elif step == "x":
            prepare()
        elif step[0] == "S":
            stat[int(step[1])].wait()
        elif step == "grad":
            grads = [
                Message(grad.at[:, columns(1 - c, j)], gt.at[j, COLS : 2 * COLS], sib) for j in range(2)
            ]
        elif step == "gw":
            for j in range(2):
                grad_copies[j].wait()
                grads[j].wait()
        else:
            for name in step:
                next(runs.get(name, iter(())), None)
    for j in tail:
        tail[j][0].wait()
    for load in loads:
        if not load.waited:
            load.wait()
    for message in sent:
        if not message.arrived:
            message.wait()
    for message in sent:
        message.copy.wait_send()


def body(hidden, down_grad, old_inverse, owner, damping):
    V = pltpu.VMEM
    any_space = pl.BlockSpec(memory_space=pl.ANY)
    smem = pl.BlockSpec(memory_space=pltpu.SMEM)
    result, inverse = pl.pallas_call(
        kernel,
        out_shape=(
            jax.ShapeDtypeStruct(down_grad.shape[::-1], BF),
            jax.ShapeDtypeStruct(old_inverse.shape, F32),
        ),
        in_specs=[smem, smem, any_space, any_space, any_space],
        out_specs=(any_space, any_space),
        scratch_shapes=[
            V((4, hidden.shape[0], B), BF),
            V((2, PACK, T), F32),
            V((2, PACK, T), BF),
            V((2, PACK, T), BF),
            V((2, 2, 4, SHARD, T), BF),
            V((2, 2, 4, SHARD, T), BF),
            V((2, SHARD, T), F32),
            V((2, SHARD, T), BF),
            V((2, SHARD, T), BF),
            V((2, PACK, T), BF),
            V((Z, 2, 2, WROWS, B), BF),
            V((WROWS, B), F32),
            V((B, B), BF),
            V((2, B, B), BF),
            V((2, B, B), BF),
            V((2, B, B), BF),
            V((2, 2 * COLS, B), BF),
            V((2 * COLS, B), BF),
            V((2 * COLS, B), F32),
            V((2 * COLS, B), BF),
            V((2, 2 * COLS, B), BF),
            V((2, 2 * COLS, B), F32),
            V((2 * WROWS, B), F32),
            V((WROWS, B), F32),
            V((WROWS, B), F32),
            pltpu.SemaphoreType.DMA((16,)),
            pltpu.SemaphoreType.DMA((N_MSG,)),
            pltpu.SemaphoreType.DMA((N_MSG,)),
        ],
        compiler_params=pltpu.CompilerParams(collective_id=0, has_side_effects=True, vmem_limit_bytes=60 << 20),
    )(owner, damping.reshape(1, 1), hidden, down_grad.T, old_inverse)
    return result.T, inverse


def solution(mesh):
    in_specs = (
        P("dp", "tensor"),
        P("tensor", "dp"),
        P("tensor", "dp", None),
        P("tensor", None),
        P(),
    )
    out_specs = (P("tensor", "dp"), P("tensor", "dp", None))
    return jax.shard_map(body, mesh=mesh, in_specs=in_specs, out_specs=out_specs, check_vma=False)
```

profile of v0, /device:TPU:1, one launch (start us, length us, event | category | flops | bytes accessed | tf_op | source)
XLA Modules:
  0.0 67.7 jit_solution(2259129737980518274)
XLA Ops:
  1.3 63.2 %shard_map.68 = (bf16[192,3072]{1,0:T(8,128)(2,1)}, f32[1,96,768]{2,1,0:T(8,128)}) custom-call(s32[1,4]{1,0:T(1,128)} %owner.1, f32[1,1]{1,0:T(1,128)} %bitcast.3.damping, bf16[512,3072]{1,0:T(8,128)(2,1)} %hid.1, bf16[192,3072]{1,0:T(8,128)(2,1)} %bitcast.4, f32[1,96,768]{2,1,0:T(8,128)} %old.1), custom_call_target="tpu_custom_call" | custom-call | tf_op jit(solution)/shard_map/pallas_call | solution.py:371
  64.5 0.0 copy-start
  64.5 2.4 %copy.10 = bf16[3072,192]{0,1:T(8,128)(2,1)} copy(bf16[3072,192]{0,1:T(8,128)(2,1)} %bitcast.5) | data formatting | bytes 2359296
  66.9 0.0 copy-done
  66.9 0.7 %copy.11 = f32[1,96,768]{2,1,0:T(8,128)} copy(f32[1,96,768]{2,1,0:T(8,128)S(1)} %copy-done) | data formatting | bytes 589824
Async XLA Ops:
  64.5 2.4 %copy-start = (f32[1,96,768]{2,1,0:T(8,128)S(1)}, f32[1,96,768]{2,1,0:T(8,128)}, u32[]{:S(2)}) copy-start(f32[1,96,768]{2,1,0:T(8,128)} %get-tuple-element.9) | copy-start | bytes 884740
where the time goes:
time: 67.8 us; the launch traced here: 67.7 us
  Pallas kernels  63.2 us (93%)
  local copies, waits for them, and re-layouts  3.12 us (5%)
  between operations  1.29 us (2%)
    pallas_call x1, Pallas kernels, body(): pl.pallas_call(kernel, out_shape=(jax.ShapeDtypeStruct(down_grad.shape[::...  63.2 us
    unnamed x4, local copies, waits for them, and re-layouts  3.12 us

commit v1 on v0

--- a/solution.py
+++ b/solution.py
@@ -17,6 +17,7 @@
 COLS = 192
 TOKENS = 16384
 N_MSG = 140
+KEEP = 30
 WARM = ((0, 48, 32), (48, 48, 16))
 BF = jnp.bfloat16
 F32 = jnp.float32
@@ -43,7 +44,7 @@
 PLAN = (
     "G0", "bar", "P0", "W", "V", "grad", "G1", "P1", "G2", "S0", "ab", "G3", "S1", "W", "ab", "cd", "V",
     "ab", "cd", "W", "ab", "cd", "V", "ab", "cd", "W", "ab", "cd", "V", "ab", "cd", "W", "V", "ab", "cd",
-    "gw", "W", "V", "ab", "cd", "x", "AA", "cd", "AAAAA", "cd", "BBB", "N", "BBBB", "N", "N",
+    "gw", "W", "V", "ab", "cd", "x", "y0", "y1", "AA", "cd", "AAAAA", "cd", "BBB", "N", "BBBB", "N", "N",
 )
 
 
@@ -68,6 +69,11 @@
     across = (z * 4 + (1 - yh) * 2 + c, tens)
     sib = (z * 4 + yh * 2 + 1 - c, tens)
     dirs = (down, up)
+
+    barrier = pltpu.get_barrier_semaphore()
+    for device in (up, down, across, sib):
+        pl.semaphore_signal(barrier, inc=1, device_id=device, device_id_type=MESH)
+
     sent = []
 
     class Message:
@@ -110,10 +116,6 @@
         return pl.ds(pl.multiple_of((2 * core + j) * B, B), B)
 
     grad_copies = [Load(grad.at[:, columns(c, j)], gt.at[j, 0:COLS], 5 + j) for j in range(2)]
-
-    barrier = pltpu.get_barrier_semaphore()
-    for device in (up, down, across, sib):
-        pl.semaphore_signal(barrier, inc=1, device_id=device, device_id_type=MESH)
 
     row = lax.broadcasted_iota(jnp.int32, (T, T), 0)
     column = lax.broadcasted_iota(jnp.int32, (T, T), 1)
@@ -247,8 +249,6 @@
         for j in range(2):
             slot = owner[0, 2 * c + j]
             x0[j] = w[pl.ds(2 * slot, 2)].reshape(B, B)
-        for j in range(2):
-            g0[j] = nt_dot(gt[j], x0[j])
 
     def refine(j):
         for name in piece_names[j]:
@@ -269,10 +269,11 @@
             rest = jnp.where(row > column, turned, last[i : i + 1, :])
             sf[at, at] = jnp.where(row < column, tile, rest).astype(BF)
         yield
-        product = dot(x0[j], sf[...])
-        diagonal = lax.broadcasted_iota(jnp.int32, (B, B), 0) == lax.broadcasted_iota(jnp.int32, (B, B), 1)
-        left = jnp.where(diagonal, 1.0, 0.0) - product * (1.0 / TOKENS) - damp * x0[j].astype(F32)
+        left = dot(x0[j], sf[...]) * (-1.0 / TOKENS) - damp * x0[j].astype(F32)
         q1[j] = left.astype(BF)
+        for i in range(NT):
+            at = slice(T * i, T * i + T)
+            q1[j, at, at] = (left[at, at] + jnp.where(row == column, 1.0, 0.0)).astype(BF)
         yield
         q2[j] = dot(q1[j], q1[j]).astype(BF)
         yield
@@ -327,6 +328,7 @@
         for name, piece in zip(piece_names[j], PIECES[j]):
             runs[name] = stream(j, *piece)
     stat = []
+    released = 0
     for step in PLAN:
         if step[0] == "G":
             gram(int(step[1]))
@@ -339,6 +341,9 @@
             w[z, yh, c] = wf[...].astype(BF)
         elif step == "x":
             prepare()
+        elif step[0] == "y":
+            j = int(step[1])
+            g0[j] = nt_dot(gt[j], x0[j])
         elif step[0] == "S":
             stat[int(step[1])].wait()
         elif step == "grad":
@@ -352,6 +357,9 @@
         else:
             for name in step:
                 next(runs.get(name, iter(())), None)
+        while len(sent) - released > KEEP:
+            sent[released].copy.wait_send()
+            released += 1
     for j in tail:
         tail[j][0].wait()
     for load in loads:
@@ -360,7 +368,7 @@
     for message in sent:
         if not message.arrived:
             message.wait()
-    for message in sent:
+    for message in sent[released:]:
         message.copy.wait_send()
 
 

time: 67.8 us -> 67.7 us (level)
  no operation moved by 1% of the time
where the time goes in v1:
time: 67.7 us; the launch traced here: 67.5 us
  Pallas kernels  63.1 us (93%)
  local copies, waits for them, and re-layouts  3.12 us (5%)
  between operations  1.29 us (2%)
    pallas_call x1, Pallas kernels, body(): pl.pallas_call(kernel, out_shape=(jax.ShapeDtypeStruct(down_grad.shape[::...  63.1 us
    unnamed x4, local copies, waits for them, and re-layouts  3.12 us

profile of v1, /device:TPU:1, one launch (start us, length us, event | category | flops | bytes accessed | tf_op | source)
XLA Modules:
  0.0 67.5 jit_solution(4467356410094336972)
XLA Ops:
  1.3 63.1 %shard_map.68 = (bf16[192,3072]{1,0:T(8,128)(2,1)}, f32[1,96,768]{2,1,0:T(8,128)}) custom-call(s32[1,4]{1,0:T(1,128)} %owner.1, f32[1,1]{1,0:T(1,128)} %bitcast.3.damping, bf16[512,3072]{1,0:T(8,128)(2,1)} %hid.1, bf16[192,3072]{1,0:T(8,128)(2,1)} %bitcast.4, f32[1,96,768]{2,1,0:T(8,128)} %old.1), custom_call_target="tpu_custom_call" | custom-call | tf_op jit(solution)/shard_map/pallas_call | solution.py:379
  64.4 0.0 copy-start
  64.4 2.4 %copy.10 = bf16[3072,192]{0,1:T(8,128)(2,1)} copy(bf16[3072,192]{0,1:T(8,128)(2,1)} %bitcast.5) | data formatting | bytes 2359296
  66.8 0.0 copy-done
  66.8 0.7 %copy.11 = f32[1,96,768]{2,1,0:T(8,128)} copy(f32[1,96,768]{2,1,0:T(8,128)S(1)} %copy-done) | data formatting | bytes 589824
Async XLA Ops:
  64.4 2.4 %copy-start = (f32[1,96,768]{2,1,0:T(8,128)S(1)}, f32[1,96,768]{2,1,0:T(8,128)}, u32[]{:S(2)}) copy-start(f32[1,96,768]{2,1,0:T(8,128)} %get-tuple-element.9) | copy-start | bytes 884740
